TPU v7x, 256 devices: a whole 4x4x8 slice. The times are simulated.
256 devices in a mesh: dp: 16 (over y_hi, z), mp: 16 (over y_lo, x, core).
Axes of the slice: x: 4, y: 4 (y_hi: 2, y_lo: 2; y = y_hi * 2 + y_lo), z: 8, core: 2. Of those that a mesh axis runs over, the one named last changes fastest.
Arguments:
- tokens: bfloat16 [32, 128, 6144], P('dp', 'mp'), may hold values from -6 to 6
- segment_ids: int32 [32, 128], P('dp'), may hold values from 0 to 3, never falling along the last dimension, each value on 1 to 64 neighbouring positions
- block_order: int32 [32], replicated, may hold values from 0 to 31, each once
- layer_norm_gain: float32 [6144], replicated, may hold values from 0.25 to 1.75
- w_proj: bfloat16 [6144, 3, 4096], P(None, None, 'mp'), as said below
- d_attended: bfloat16 [4096, 4096], P('dp', 'mp'), may hold values from -6 to 6
Outputs:
- attended: bfloat16 [4096, 4096], P('dp', 'mp')
- token_block_gradient: bfloat16 [32, 128, 6144], P('dp', 'mp')
- d_proj: bfloat16 [6144, 3, 4096], P('dp', None, 'mp')
- norm_gain_gradient: float32 [6144], replicated
Inputs may be any that keep to these rules, and one draw needn't show every extreme that they name: `segment_ids`: within each block the ids never fall and number its images from 0. `block_order`: each block number appears once. `w_proj`: entries are at most 6 / sqrt(6144) in magnitude.
All inputs are finite; a program needn't handle non-finite values.
Results may differ from a plain program's by a relative error of at most 0.025.
The roundings to bfloat16 on the way count: a program that leaves them out, or rounds other values in their place, can miss the bound.
Values may be sent and summed in bfloat16 or wider, within the bound.
A program may use at most 128 MiB of HBM per device.

v0:
```python
import jax
import jax.numpy as jnp
from jax import lax
from jax.sharding import PartitionSpec as P

HD = 128


def layer_statistics(rows):
    center = rows - jnp.mean(rows, axis=-1, keepdims=True)
    inverse_deviation = lax.rsqrt(jnp.mean(center * center, axis=-1, keepdims=True) + 1e-06)
    return (center * inverse_deviation, inverse_deviation)


def attend_forward(query, keys, values, segs):
    scale = HD ** (-0.5)
    scores = jnp.einsum("bqhd,bkhd->bhqk", query, keys, preferred_element_type=jnp.float32) * scale
    same = (segs[:, :, None] == segs[:, None, :])[:, None]
    scores = jnp.where(same, scores, -1e30)
    peak = jnp.max(scores, axis=-1, keepdims=True)
    expo = jnp.exp(scores - peak)
    probs = expo / jnp.sum(expo, axis=-1, keepdims=True)
    probs_b = probs.astype(jnp.bfloat16)
    out = jnp.einsum("bhqk,bkhd->bqhd", probs_b, values, preferred_element_type=jnp.float32)
    return (out.astype(jnp.bfloat16), probs, probs_b)


def attend_backward(query, keys, values, probs, probs_b, grad_out):
    scale = HD ** (-0.5)
    dprob = jnp.einsum("bqhd,bkhd->bhqk", grad_out, values, preferred_element_type=jnp.float32)
    dvalue = jnp.einsum("bhqk,bqhd->bkhd", probs_b, grad_out, preferred_element_type=jnp.float32)
    delta = jnp.sum(probs * dprob, axis=-1, keepdims=True)
    dscore = (probs * (dprob - delta)).astype(jnp.bfloat16)
    dquery = jnp.einsum("bhqk,bkhd->bqhd", dscore, keys, preferred_element_type=jnp.float32) * scale
    dkey = jnp.einsum("bhqk,bqhd->bkhd", dscore, query, preferred_element_type=jnp.float32) * scale
    return jnp.stack([dquery, dkey, dvalue], axis=2).astype(jnp.bfloat16)


def per_device(tokens, segment_ids, block_order, layer_norm_gain, w_proj, d_attended):
    groups = tokens.shape[0]
    wanted = lax.dynamic_slice_in_dim(block_order, lax.axis_index("dp") * groups, groups)
    seg_acc = jnp.zeros(segment_ids.shape, jnp.int32)
    part_rows = lax.all_gather(tokens, "dp", axis=0, tiled=True)
    part_segs = lax.all_gather(segment_ids, "dp", axis=0, tiled=True)
    count = part_rows.shape[0]
    picks = wanted[:, None] == jnp.arange(count, dtype=jnp.int32)[None, :]
    row_accumulator = jnp.einsum(
        "bn,nrd->brd", picks.astype(jnp.bfloat16), part_rows, preferred_element_type=jnp.float32
    )
    seg_acc = seg_acc + jnp.sum(jnp.where(picks[:, :, None], part_segs[None], 0), axis=1)
    centered_input_local, local_inverse_deviation = layer_statistics(row_accumulator)
    outgoing = row_accumulator.astype(jnp.bfloat16)
    complete_tokens = lax.all_gather(outgoing, "mp", axis=1, tiled=True)
    centered_input_total, discarded_inverse_deviation = layer_statistics(
        complete_tokens.astype(jnp.float32)
    )
    normalized_input = (centered_input_total * layer_norm_gain).astype(jnp.bfloat16)
    proj = jnp.einsum(
        "btd,dcf->btcf", normalized_input, w_proj, preferred_element_type=jnp.float32
    ).astype(jnp.bfloat16)
    blen = proj.shape[1]
    width = proj.shape[3]
    heads = width // HD
    split = proj.reshape(groups, blen, 3, heads, HD)
    query, keys, values = (split[:, :, 0], split[:, :, 1], split[:, :, 2])
    out, probs, probs_b = attend_forward(query, keys, values, seg_acc)
    attended = out.reshape(groups * blen, width)
    grad_out = d_attended.reshape(groups, blen, heads, HD)
    dqkv = attend_backward(query, keys, values, probs, probs_b, grad_out).reshape(
        groups, blen, 3, width
    )
    part = normalized_input
    d_proj = lax.psum_scatter(
        jnp.einsum("btd,btcf->dcf", part, dqkv, preferred_element_type=jnp.float32).astype(
            jnp.bfloat16
        ),
        "dp",
        scatter_dimension=0,
        tiled=True,
    )
    part = dqkv
    summed = lax.psum_scatter(
        jnp.einsum("brcf,dcf->rbd", part, w_proj, preferred_element_type=jnp.float32).astype(
            jnp.bfloat16
        ),
        "mp",
        scatter_dimension=0,
        tiled=True,
    ).astype(jnp.float32)
    normalized_gradient = jnp.swapaxes(summed, 0, 1)
    norm_gain_gradient = lax.psum(
        jnp.sum(normalized_gradient * centered_input_local, axis=(0, 1)), ("dp", "mp")
    )
    gain_scaled = normalized_gradient * layer_norm_gain
    token_block_gradient = local_inverse_deviation * (
        gain_scaled
        - jnp.mean(gain_scaled, axis=-1, keepdims=True)
        - centered_input_local
        * jnp.mean(gain_scaled * centered_input_local, axis=-1, keepdims=True)
    )
    return (attended, token_block_gradient.astype(jnp.bfloat16), d_proj, norm_gain_gradient)


def solution(mesh):
    placed = (P("dp", "mp", None), P("dp", None), P(), P(), P(None, None, "mp"), P("dp", "mp"))
    return jax.shard_map(
        per_device,
        mesh=mesh,
        in_specs=placed,
        out_specs=(P("dp", "mp"), P("dp", "mp", None), P("dp", None, "mp"), P()),
        check_vma=False,
    )
```

profile of v0, /device:TPU:8, one launch (start us, length us, event | category | flops | bytes accessed | tf_op | source)
XLA Modules:
  0.0 577.0 jit_solution(8446972053322522390)
XLA Ops:
  7.2 0.7 all-gather.4.cloned.1.call-update
  7.9 0.0 all-gather.6.cloned.1.call-start
  7.9 0.7 dynamic_slice.3
  8.7 97.2 %all-gather.4.cloned.1.call-done = bf16[32,8,6144]{2,1,0:T(8,128)(2,1)} async-done(((bf16[2,8,6144]{2,1,0:T(8,128)(2,1)}), bf16[32,8,6144]{2,1,0:T(8,128)(2,1)}) %all-gather.4.cloned.1.call-update) | async-done | bytes 3145744 | tf_op jit(solution)/shard_map/all_gather | solution.py:43
  105.9 5.4 fusion.53
  111.3 1.1 multiply_reduce_fusion
  112.4 0.0 all-reduce.3.cloned.1.call-start
  112.5 0.9 reshape.89
  113.4 0.8 copy.127
  114.2 38.5 %all-gather = s32[16,2,128]{2,1,0:T(2,128)S(1)} all-gather(s32[1,2,128]{2,1,0:T(2,128)} %bitcast.115), channel_id=1, replica_groups=mesh['dp'=16,'mp'=16] {'dp'}, dimensions={0}, use_global_device_ids=true | all-gather | bytes 17408 | tf_op jit(solution)/shard_map/all_gather | solution.py:44
  152.6 0.1 iota_compare_fusion
  152.7 0.1 select_reduce_fusion
  152.8 0.7 broadcast_compare_fusion
  153.5 2.9 convert_reduce_fusion
  156.5 3.6 fusion.16
  160.1 0.6 copy-done.5
  160.7 8.5 %fusion.24 = bf16[2,128,3,256]{3,1,2,0:T(8,128)(2,1)} fusion(bf16[6144,3,256]{2,0,1:T(8,128)(2,1)} %param.10, f32[6144]{0:T(1024)S(1)} %copy-done.3, f32[2,128]{1,0:T(2,128)S(1)} %add_rsqrt_fusion.1, f32[2,128]{1,0:T(2,128)S(1)} %broadcast_multiply_fusion.3, bf16[2,128,6144]{2,0,1:T(2,128)(2,1)S(1)} %copy-done), kind=kOutput, calls=%fused_computation.19 | convolution fusion | flops 2423980032 | bytes 13002752 | tf_op jit(solution)/shard_map/btd,dcf->btcf/dot_general | solution.py:58
  169.2 1.8 reshape.87
  171.0 2.0 fusion.52
  173.0 1.7 copy.149
  174.7 1.2 fusion.30
  175.9 0.7 copy-done.1
  176.6 0.8 fusion.54
  177.3 2.0 convolution_convert_fusion
  179.3 1.3 multiply_reduce_fusion.1
  180.6 1.0 multiply_convert_fusion
  181.6 1.7 fusion.34
  183.4 1.8 fusion.35
  185.2 1.7 copy.130
  186.8 1.7 copy.121
  188.5 1.7 copy.128
  190.1 1.7 copy.125
  191.8 1.7 copy.129
  193.5 6.5 %fusion.13 = bf16[128,2,6144]{2,0,1:T(8,128)(2,1)S(1)} fusion(bf16[6144,3,256]{2,0,1:T(8,128)(2,1)} %param.10, bf16[2,128,1,256]{3,1,2,0:T(8,128)(2,1)} %copy.130, bf16[2,128,1,256]{3,1,2,0:T(8,128)(2,1)} %copy.129, bf16[2,128,1,256]{3,1,2,0:T(8,128)(2,1)} %copy.128), kind=kOutput, calls=%fused_computation.12 | convolution fusion | flops 2417885184 | bytes 12976128 | tf_op jit(solution)/shard_map/brcf,dcf->rbd/dot_general | solution.py:83
  200.0 5.1 copy.131
  205.2 0.0 reduce-scatter.2.cloned.1.call-start
  205.2 7.5 %bitcast_convert_fusion = bf16[6144,3,256]{2,0,1:T(8,128)(2,1)} fusion(f32[6144]{0:T(1024)} %param.9, f32[2,128]{1,0:T(2,128)} %copy-done.5, f32[2,128]{1,0:T(2,128)S(1)} %broadcast_multiply_fusion.3, bf16[2,128,6144]{2,0,1:T(2,128)(2,1)S(1)} %copy-done, bf16[2,128,1,256]{3,1,2,0:T(8,128)(2,1)} %copy.130, bf16[2,128,1,256]{3,1,2,0:T(8,128)(2,1)} %copy.129, ...), kind=kOutput, calls=%fused_computation.1 | convolution fusion | flops 2429681664 | bytes 13002752 | tf_op jit(solution)/shard_map/btd,btcf->dcf/dot_general | solution.py:74
  212.8 0.6 copy-done.6
  213.5 0.6 dynamic-slice
  214.7 1.3 fusion.36
  216.0 0.1 copy.115
  216.1 0.7 copy.171
  216.8 115.3 %all-reduce.3.cloned.1.call-done = bf16[128,2,6144]{2,1,0:T(2,128)(2,1)} async-done(((bf16[128,2,6144]{2,1,0:T(2,128)(2,1)}), bf16[128,2,6144]{2,1,0:T(2,128)(2,1)}) %all-reduce.3.cloned.1.call-update) | async-done | bytes 3145744
  332.1 1.7 fusion.43
  333.8 1.4 fusion.44
  335.3 0.7 copy.134
  336.0 82.4 %psum.7 = f32[6144]{0:T(1024)} all-reduce(f32[6144]{0:T(1024)S(1)} %get-tuple-element.24), channel_id=1, replica_groups=mesh['dp'=16,'mp'=16] {'dp','mp'}, use_global_device_ids=true, to_apply=%region_13.14 | all-reduce | flops 6144 | bytes 49152 | tf_op jit(solution)/shard_map/psum | solution.py:91
  418.4 152.0 %reduce-scatter.2.cloned.1.call-done = bf16[384,3,256]{2,0,1:T(8,128)(2,1)} async-done(((bf16[6144,3,256]{2,0,1:T(8,128)(2,1)}), bf16[384,3,256]{2,0,1:T(8,128)(2,1)}) %reduce-scatter.2.cloned.1.call-update) | async-done | bytes 589840 | tf_op jit(solution)/shard_map/reduce_scatter | solution.py:73
  (21 shorter events, 0.1 us)
Async XLA Ops:
  7.2 98.7 %all-gather.4.cloned.1.call-start = ((), (), s32[]{:S(2)}) async-start(), calls=%async_computation.1 | async-start | bytes 3342336 | tf_op jit(solution)/shard_map/all_gather | solution.py:43
  7.9 145.6 %all-gather.6.cloned.1.call-start = ((), (), s32[]{:S(2)}) async-start(), calls=%async_computation.2 | async-start | bytes 3342336 | tf_op jit(solution)/shard_map/all_gather | solution.py:53
  112.4 219.7 %all-reduce.3.cloned.1.call-start = ((), (), s32[]{:S(2)}) async-start(), calls=%async_computation.4 | async-start | bytes 6291456
  153.5 7.1 %copy-start = (bf16[2,128,6144]{2,0,1:T(2,128)(2,1)S(1)}, bf16[2,128,6144]{2,0,1:T(2,128)(2,1)}, u32[]{:S(2)}) copy-start(bf16[2,128,6144]{2,0,1:T(2,128)(2,1)} %all-gather.6.cloned.1.call-done) | copy-start | bytes 9437188
  153.5 7.1 %copy-start.3 = (f32[6144]{0:T(1024)S(1)}, f32[6144]{0:T(1024)}, u32[]{:S(2)}) copy-start(f32[6144]{0:T(1024)} %param.9) | copy-start | bytes 73732
  160.1 0.6 copy-start.5
  175.8 0.7 copy-start.1
  205.2 365.2 %reduce-scatter.2.cloned.1.call-start = ((), (), s32[]{:S(2)}) async-start(), calls=%async_computation.3 | async-start | bytes 10027008 | tf_op jit(solution)/shard_map/reduce_scatter | solution.py:73
  212.8 0.7 copy-start.6
  212.8 1.9 copy-start.2
  212.8 119.3 %copy-start.4 = (f32[6144]{0:T(1024)S(1)}, f32[6144]{0:T(1024)}, u32[]{:S(2)}) copy-start(f32[6144]{0:T(1024)} %param.9) | copy-start | bytes 73732
Sparse Core Ops, SparseCore 0:
  10.6 95.2 all-gather.3
  112.5 35.5 all-gather.5
  205.3 126.7 all-reduce.2
  336.7 233.6 reduce-scatter.1
where the time goes:
time: 579 us; the launch traced here: 577 us
  waiting for transfers between devices  365 us (63%)
  blocking collectives  121 us (21%)
  matrix products  37.3 us (6%)
  local copies, waits for them, and re-layouts  25.4 us (4%)
  between operations  14.5 us (3%)
  other arithmetic  13.5 us (2%)
    reduce_scatter x1, waiting for transfers between devices, per_device(): lax.psum_scatter(jnp.einsum('btd,btcf->dcf', part, dqkv, preferred_elemen...  152 us
    unnamed x5, waiting for transfers between devices  116 us
    all_gather x1, waiting for transfers between devices, per_device(): part_rows = lax.all_gather(tokens, 'dp', axis=0, tiled=True)  97.2 us
    psum x1, blocking collectives, per_device(): lax.psum(jnp.sum(normalized_gradient * centered_input_local, axis=(0, 1))...  82.4 us
    all_gather x1, blocking collectives, per_device(): part_segs = lax.all_gather(segment_ids, 'dp', axis=0, tiled=True)  38.5 us
  transfers between devices with their start and end apart: 4, of which 3 were waited for; matrix products, arithmetic and copies ran while one was open for 3% of the time, Pallas kernels for 0%

commit v1 on v0

v1 whole, which is shorter than its diff:
```python
import jax
import jax.numpy as jnp
from jax import lax
from jax.experimental import pallas as pl
from jax.experimental.pallas import tpu as pltpu
from jax.sharding import PartitionSpec as P

D = 6144
HD = 128
PC = 384
NP = 16
F32 = jnp.float32
BF16 = jnp.bfloat16
MESH = pl.DeviceIdType.MESH
ORDER = (2, 0, 1)


def dot(a, b, ca=1, cb=0):
    return lax.dot_general(a, b, (((ca,), (cb,)), ((), ())), preferred_element_type=F32)


def hops_of(way, head):
    return 4 if way == head else 3


def kernel(
    order, tok, seg, gain, w_hbm, datt,
    att_o, tbg_o, dproj_o, gg_o,
    wv, r1, r2s, r2, segp, sega, gat, nsb, xh, proj, zb, nt, dnb, rsa, b1, rsb, b2, rsc,
    acc, ysnd, rl, fin, gp, g1, g2s, g2, g3s, g3,
    wsem, lsem, r1sem, r2sem, sgsem, nasem, gasem, nssem, zsem, rasem, rbsem, rcsem, ysem,
    g1sem, g2sem, g3sem,
):
    dp = lax.axis_index("dp")
    mp = lax.axis_index("mp")
    yh, z = dp // 8, dp % 8
    yl, x, core = mp // 8, (mp // 2) % 4, mp % 2

    def mpid(a, b, c):
        return a * 8 + b * 2 + c

    def mp_of(slot):
        return mpid((slot // 4) % 2, slot % 4, slot // 8)

    sg = core * 8 + yl * 4 + x
    sib = (dp, mpid(yl, x, 1 - core))
    yn = (dp, mpid(1 - yl, x, core))
    xp = (dp, mpid(yl, (x + 1) % 4, core))
    xm = (dp, mpid(yl, (x + 3) % 4, core))
    xo = (dp, mpid(yl, (x + 2) % 4, core))
    zp = (yh * 8 + (z + 1) % 8, mp)
    zm = (yh * 8 + (z + 7) % 8, mp)
    yup_h = jnp.where(yl == 0, yh, 1 - yh)
    ydn_h = jnp.where(yl == 1, yh, 1 - yh)
    yup = (yup_h * 8 + z, mpid(1 - yl, x, core))
    ydn = (ydn_h * 8 + z, mpid(1 - yl, x, core))
    far = ((1 - yh) * 8 + z, mpid(1 - yl, x, core))

    def rc(src, dst, sems, dev):
        ss, rs = sems
        return pltpu.make_async_remote_copy(
            src_ref=src, dst_ref=dst, send_sem=ss, recv_sem=rs, device_id=dev, device_id_type=MESH
        )

    pend = []

    def send(src, dst, sems, dev):
        rc(src, dst, sems, dev).start()
        pend.append((src, dst, sems, dev))

    def got(dst, sems):
        rc(dst, dst, sems, sib).wait_recv()

    wcp = [
        pltpu.make_async_copy(
            w_hbm.at[:, pl.ds(k * 1536, 1536)], wv.at[:, pl.ds(k * 1536, 1536)], wsem.at[k]
        )
        for k in range(4)
    ]
    for cp in wcp:
        cp.start()

    barrier = pltpu.get_barrier_semaphore()

    def greet(i, _):
        pl.semaphore_signal(barrier, inc=1, device_id=((dp + i) % 16, mp), device_id_type=MESH)
        pl.semaphore_signal(
            barrier, inc=1, device_id=(dp, mp_of((sg + i) % 16)), device_id_type=MESH
        )
        return _

    lax.fori_loop(1, 16, greet, 0)
    pl.semaphore_signal(barrier, inc=1, device_id=far, device_id_type=MESH)
    segp[...] = jnp.zeros_like(segp)
    segp[0:2, :] = seg[...]
    pl.semaphore_wait(barrier, 31)

    def cols(j):
        return pl.ds(pl.multiple_of(j * PC, 128), PC)

    def r1_copy(i):
        d = (dp + i) % 16
        return rc(tok.at[:, cols(d)], r1.at[dp], (r1sem.at[0, i], r1sem.at[1, i]), (d, mp))

    def sg_copy(i):
        d = (dp + i) % 16
        return rc(segp, sega.at[dp], (sgsem.at[0, i], sgsem.at[1, i]), (d, mp))

    def r1_send(i, _):
        r1_copy(i).start()
        return _

    def sg_send(i, _):
        sg_copy(i).start()
        return _

    lax.fori_loop(1, 16, r1_send, 0)
    lax.fori_loop(1, 16, sg_send, 0)
    own = pltpu.make_async_copy(tok.at[:, cols(dp)], r1.at[dp], lsem.at[0])
    own.start()
    sega[dp] = segp[...]

    def source(i):
        s, b, r = i >> 4, (i >> 3) & 1, i & 7
        m = ((s >> 2) & 1) * 8 + (s & 3) * 2 + (s >> 3)
        return b * 128 + m * 8 + r

    ri = lax.broadcasted_iota(jnp.int32, (256, 256), 0)
    ci = lax.broadcasted_iota(jnp.int32, (256, 256), 1)
    perm = jnp.where(source(ri) == ci, 1.0, 0.0).astype(BF16)
    perm_t = jnp.where(source(ci) == ri, 1.0, 0.0).astype(BF16)
    g = dot(perm, datt[...]).astype(BF16)

    own.wait()

    def r1_wait(i, _):
        s = (dp + 16 - i) % 16
        got(r1.at[s], (r1sem.at[0, i], r1sem.at[1, i]))
        return _

    lax.fori_loop(1, 16, r1_wait, 0)

    def half_of(p):
        b = order[p]
        t = r1[b >> 1].astype(F32)
        return jnp.where((b & 1) == 1, t[8:16], t[0:8])

    def pick(d):
        return jnp.concatenate([half_of(2 * d), half_of(2 * d + 1)], axis=0).astype(BF16)

    def r2_copy(i):
        d = (dp + i) % 16
        return rc(r2s.at[d], r2.at[dp], (r2sem.at[0, i], r2sem.at[1, i]), (d, mp))

    def r2_send(i, _):
        d = (dp + i) % 16
        r2s[d] = pick(d)
        r2_copy(i).start()
        return _

    lax.fori_loop(1, 16, r2_send, 0)
    r2[dp] = pick(dp)

    def sg_wait(i, _):
        s = (dp + 16 - i) % 16
        got(sega.at[s], (sgsem.at[0, i], sgsem.at[1, i]))
        return _

    lax.fori_loop(1, 16, sg_wait, 0)

    def ids_of(p):
        b = order[p]
        t = sega[b >> 1].astype(F32)
        return jnp.where((b & 1) == 1, t[1:2], t[0:1])

    ids = jnp.concatenate([ids_of(2 * dp), ids_of(2 * dp + 1) + 4.0], axis=1)
    ids = jnp.broadcast_to(ids, (8, 256)).astype(BF16)
    id_row = dot(ids, perm_t)[0:1]
    id_col = dot(perm, ids, 1, 1)[:, 0:1]
    same = id_col == id_row

    def r2_wait(i, _):
        s = (dp + 16 - i) % 16
        got(r2.at[s], (r2sem.at[0, i], r2sem.at[1, i]))
        return _

    lax.fori_loop(1, 16, r2_wait, 0)

    rows = r2[...].astype(F32)
    mean = jnp.sum(jnp.sum(rows, axis=0), axis=-1, keepdims=True) * (1.0 / D)
    cen = rows - mean[None]
    var = jnp.sum(jnp.sum(cen * cen, axis=0), axis=-1, keepdims=True) * (1.0 / D)
    rstd = lax.rsqrt(var + 1e-06)
    xhat = cen * rstd[None]
    xh[...] = xhat
    for j in range(NP):
        gat[j, sg] = (xhat[j] * gain[j : j + 1, :]).astype(BF16)

    def gather(buf, sems):
        def at(k, slot):
            return buf.at[pl.ds(4 * k, 4), slot]

        def slot(a, b):
            return core * 8 + a * 4 + b

        def sm(k, n):
            return (sems.at[0, k, n], sems.at[1, k, n])

        def go(k, a, b, n, dev):
            ref = at(k, slot(a, b))
            send(ref, ref, sm(k, n), dev)

        def have(k, a, b, n):
            got(at(k, slot(a, b)), sm(k, n))

        x1, x2, x3 = (x + 1) % 4, (x + 2) % 4, (x + 3) % 4

        def stage1(k):
            go(k, yl, x, 0, yn)
            go(k, yl, x, 1, xp)
            go(k, yl, x, 2, xm)

        def stage2(k):
            have(k, 1 - yl, x, 0)
            go(k, 1 - yl, x, 3, xp)
            go(k, 1 - yl, x, 4, xm)

        def stage3(k):
            have(k, yl, x3, 1)
            go(k, yl, x3, 5, xp)
            have(k, 1 - yl, x1, 4)
            go(k, 1 - yl, x1, 6, xm)

        def stage4(k):
            have(k, yl, x1, 2)
            have(k, 1 - yl, x3, 3)
            have(k, yl, x2, 5)
            have(k, 1 - yl, x2, 6)
            ref = buf.at[pl.ds(4 * k, 4), pl.ds(core * 8, 8)]
            send(ref, ref, sm(k, 7), sib)

        def stage5(k):
            got(buf.at[pl.ds(4 * k, 4), pl.ds((1 - core) * 8, 8)], sm(k, 7))

        return stage1, stage2, stage3, stage4, stage5

    G1, G2, G3, G4, G5 = gather(gat, gasem)
    N1, N2, N3, N4, N5 = gather(nsb, nssem)
    for k in range(4):
        G1(k)

    def na_copy(i, o):
        t = (z + o) % 8
        return rc(
            gat.at[i * 8 + t, sg], nsb.at[i * 8 + z, sg],
            (nasem.at[0, i, o], nasem.at[1, i, o]), (yh * 8 + t, mp),
        )

    def na_send(o, _):
        na_copy(0, o).start()
        na_copy(1, o).start()
        return _

    lax.fori_loop(1, 8, na_send, 0)
    for i in range(2):
        nsb[i * 8 + z, sg] = gat[i * 8 + z, sg]

    def na_wait(o, _):
        s = (z + 8 - o) % 8
        for i in range(2):
            got(nsb.at[i * 8 + s, sg], (nasem.at[0, i, o], nasem.at[1, i, o]))
        return _

    for k in range(4):
        G2(k)
    lax.fori_loop(1, 8, na_wait, 0)
    for k in range(4):
        G3(k)
    for k in range(4):
        N1(k)
    for k in range(4):
        G4(k)
    for k in range(4):
        G5(k)
        wcp[k].wait()
        for q in range(2):
            j = 4 * k + 2 * q
            lhs = jnp.concatenate(
                [gat[j].reshape(256, PC), gat[j + 1].reshape(256, PC)], axis=1
            )
            for c in range(3):
                t = dot(lhs, wv[c, j * PC : (j + 2) * PC, :])
                proj[c] = t if j == 0 else proj[c] + t
        N2(k)

    scale = HD ** (-0.5)

    def zat(s, c, h):
        return zb.at[s, c, h]

    def z_send(way, hop, c, h):
        s = (z + (8 - hop if way == 0 else hop)) % 8
        ref = zat(s, c, h)
        send(
            ref, ref, (zsem.at[0, way, hop, c, h], zsem.at[1, way, hop, c, h]),
            zp if way == 0 else zm,
        )

    def z_have(way, hop, c, h):
        s = (z + (8 - hop if way == 0 else hop)) % 8
        got(zat(s, c, h), (zsem.at[0, way, hop - 1, c, h], zsem.at[1, way, hop - 1, c, h]))

    outs = []
    for h in range(2):
        lanes = slice(h * HD, (h + 1) * HD)
        q, k, v = [proj[c, :, lanes].astype(BF16) for c in range(3)]
        gh = g[:, lanes]
        s = jnp.where(same, dot(q, k, 1, 1) * scale, -1e30)
        e = jnp.exp(s - jnp.max(s, axis=-1, keepdims=True))
        probs = e / jnp.sum(e, axis=-1, keepdims=True)
        pb = probs.astype(BF16)

        def put(c, val):
            zb[z, c, h] = val.astype(BF16)
            z_send(0, 0, c, h)
            z_send(1, 0, c, h)

        put(2, dot(pb, gh, 0, 0))
        dprob = dot(gh, v, 1, 1)
        delta = jnp.sum(probs * dprob, axis=-1, keepdims=True)
        ds = (probs * (dprob - delta)).astype(BF16)
        put(0, dot(ds, k) * scale)
        put(1, dot(ds, q, 0, 0) * scale)
        outs.append(dot(pb, v).astype(BF16))
    att_o[...] = dot(perm_t, jnp.concatenate(outs, axis=1)).astype(BF16)

    dq = [jnp.concatenate([zb[z, c, 0], zb[z, c, 1]], axis=1) for c in range(3)]

    def dn_step(k):
        def body(j, _):
            at = pl.ds(pl.multiple_of(j * PC, 128), PC)
            t = dot(dq[0], wv[0, at, :], 1, 1)
            t = t + dot(dq[1], wv[1, at, :], 1, 1)
            t = t + dot(dq[2], wv[2, at, :], 1, 1)
            dnb[j] = t.astype(BF16).reshape(16, 16, PC)
            return _

        lax.fori_loop(4 * k, 4 * k + 4, body, 0)
        send(
            dnb.at[pl.ds(4 * k, 4), pl.ds((1 - core) * 8, 8)], rsa.at[pl.ds(4 * k, 4)],
            (rasem.at[0, k], rasem.at[1, k]), sib,
        )

    def s2(k):
        got(rsa.at[pl.ds(4 * k, 4)], (rasem.at[0, k], rasem.at[1, k]))
        for j in range(4 * k, 4 * k + 4):
            mine = dnb[j, pl.ds(core * 8, 8)].astype(F32)
            b1[j] = (mine + rsa[j].astype(F32)).astype(BF16)
        send(
            b1.at[pl.ds(4 * k, 4), pl.ds((1 - yl) * 4, 4)], rsb.at[pl.ds(4 * k, 4)],
            (rbsem.at[0, k], rbsem.at[1, k]), yn,
        )

    def s3(k):
        got(rsb.at[pl.ds(4 * k, 4)], (rbsem.at[0, k], rbsem.at[1, k]))
        for j in range(4 * k, 4 * k + 4):
            mine = b1[j, pl.ds(yl * 4, 4)].astype(F32)
            b2[j] = (mine + rsb[j].astype(F32)).astype(BF16)
        for o, dev in ((1, xp), (2, xo), (3, xm)):
            send(
                b2.at[pl.ds(4 * k, 4), (x + o) % 4], rsc.at[o - 1, pl.ds(4 * k, 4)],
                (rcsem.at[0, o, k], rcsem.at[1, o, k]), dev,
            )

    def w(hop, c):
        for way in range(2):
            for h in range(2):
                n = hops_of(way, h)
                if hop <= n:
                    z_have(way, hop, c, h)
                if hop < n:
                    z_send(way, hop, c, h)

    v_, q_, k_ = ORDER
    for k in range(4):
        N3(k)
    dn_step(0)
    dn_step(1)
    w(1, v_)
    dn_step(2)
    dn_step(3)
    w(1, q_)
    s2(0)
    s2(1)
    w(1, k_)
    s2(2)
    s2(3)
    w(2, v_)
    for k in range(4):
        N4(k)
    w(2, q_)
    s3(0)
    s3(1)
    w(2, k_)
    s3(2)
    s3(3)
    w(3, v_)
    for k in range(4):
        N5(k)

    def turn(s, _):
        for i in range(2):
            nt[s, i] = nsb[i * 8 + s].reshape(256, PC).T
        return _

    lax.fori_loop(0, 8, turn, 0)
    w(3, q_)
    w(3, k_)

    total = jnp.zeros((NP, 16, PC), F32)
    for k in range(4):
        for o in range(1, 4):
            got(rsc.at[o - 1, pl.ds(4 * k, 4)], (rcsem.at[0, o, k], rcsem.at[1, o, k]))
    xhat = xh[...]
    parts = []
    for j in range(NP):
        t = b2[j, x].astype(F32)
        for o in range(3):
            t = t + rsc[o, j].astype(F32)
        p = t * xhat[j]
        gp[j] = p[0:8] + p[8:16]
        parts.append(t * gain[j : j + 1, :])

    def g1_copy(i):
        s = (sg + i) % 16
        return rc(gp.at[s], g1.at[sg], (g1sem.at[0, i], g1sem.at[1, i]), (dp, mp_of(s)))

    def g1_send(i, _):
        g1_copy(i).start()
        return _

    lax.fori_loop(1, 16, g1_send, 0)
    g1[sg] = gp[sg]
    m1 = sum(jnp.sum(parts[j], axis=-1, keepdims=True) for j in range(NP)) * (1.0 / D)
    m2 = sum(jnp.sum(parts[j] * xhat[j], axis=-1, keepdims=True) for j in range(NP)) * (1.0 / D)
    for j in range(NP):
        t = rstd * (parts[j] - m1 - xhat[j] * m2)
        tbg_o[:, j * PC : (j + 1) * PC] = t.astype(BF16)

    def dproj(c):
        acc[c] = jnp.zeros((2, PC, 256), F32)

        def body(s, _):
            rhs = jnp.concatenate([zb[s, c, 0], zb[s, c, 1]], axis=1)
            for i in range(2):
                acc[c, i] += dot(nt[s, i], rhs)
            return _

        lax.fori_loop(0, 8, body, 0)
        ysnd[c] = acc[c, 1 - yh].astype(BF16)
        send(ysnd.at[c, pl.ds(0, 192)], rl.at[c, 0], (ysem.at[0, c, 0], ysem.at[1, c, 0]), yup)
        send(ysnd.at[c, pl.ds(192, 192)], rl.at[c, 1], (ysem.at[0, c, 1], ysem.at[1, c, 1]), ydn)

    def relay(c):
        for n, dev in ((0, yup), (1, ydn)):
            got(rl.at[c, n], (ysem.at[0, c, n], ysem.at[1, c, n]))
            send(
                rl.at[c, n], fin.at[c, pl.ds(192 * n, 192)],
                (ysem.at[0, c, 2 + n], ysem.at[1, c, 2 + n]), dev,
            )

    def finish(c):
        for n in range(2):
            got(fin.at[c, pl.ds(192 * n, 192)], (ysem.at[0, c, 2 + n], ysem.at[1, c, 2 + n]))
        dproj_o[c] = (acc[c, yh] + fin[c].astype(F32)).astype(BF16)

    w(4, v_)
    dproj(v_)

    def g1_wait(i, _):
        s = (sg + 16 - i) % 16
        got(g1.at[s], (g1sem.at[0, i], g1sem.at[1, i]))
        return _

    lax.fori_loop(1, 16, g1_wait, 0)
    t = jnp.sum(jnp.sum(g1[...], axis=0), axis=0, keepdims=True)
    g2s[...] = jnp.broadcast_to(t, (8, PC))

    def g2_copy(i):
        d = (dp + i) % 16
        return rc(g2s, g2.at[dp], (g2sem.at[0, i], g2sem.at[1, i]), (d, mp))

    def g2_send(i, _):
        g2_copy(i).start()
        return _

    lax.fori_loop(1, 16, g2_send, 0)
    g2[dp] = g2s[...]
    w(4, q_)
    dproj(q_)
    relay(v_)

    def g2_wait(i, _):
        s = (dp + 16 - i) % 16
        got(g2.at[s], (g2sem.at[0, i], g2sem.at[1, i]))
        return _

    lax.fori_loop(1, 16, g2_wait, 0)
    g3s[...] = jnp.sum(g2[...], axis=0)

    def g3_copy(i):
        s = (sg + i) % 16
        return rc(g3s, g3.at[sg], (g3sem.at[0, i], g3sem.at[1, i]), (dp, mp_of(s)))

    def g3_send(i, _):
        g3_copy(i).start()
        return _

    lax.fori_loop(1, 16, g3_send, 0)
    g3[sg] = g3s[...]
    w(4, k_)
    dproj(k_)
    relay(q_)
    finish(v_)
    relay(k_)

    def g3_wait(i, _):
        s = (sg + 16 - i) % 16
        got(g3.at[s], (g3sem.at[0, i], g3sem.at[1, i]))
        return _

    lax.fori_loop(1, 16, g3_wait, 0)
    for s in range(NP):
        gg_o[s : s + 1, :] = g3[s, 0:1, :]
    finish(q_)
    finish(k_)

    def drain(i, _):
        r1_copy(i).wait_send()
        sg_copy(i).wait_send()
        r2_copy(i).wait_send()
        g1_copy(i).wait_send()
        g2_copy(i).wait_send()
        g3_copy(i).wait_send()
        return _

    lax.fori_loop(1, 16, drain, 0)

    def drain_na(o, _):
        na_copy(0, o).wait_send()
        na_copy(1, o).wait_send()
        return _

    lax.fori_loop(1, 8, drain_na, 0)
    for item in pend:
        rc(*item).wait_send()


def per_device(tokens, segment_ids, block_order, layer_norm_gain, w_proj, d_attended):
    vm = pl.BlockSpec(memory_space=pltpu.VMEM)
    dma = pltpu.SemaphoreType.DMA
    V = pltpu.VMEM
    big = (NP, 16, 16, PC)
    att, tbg, dproj, gg = pl.pallas_call(
        kernel,
        out_shape=(
            jax.ShapeDtypeStruct((256, 256), BF16),
            jax.ShapeDtypeStruct((16, D), BF16),
            jax.ShapeDtypeStruct((3, PC, 256), BF16),
            jax.ShapeDtypeStruct((NP, PC), F32),
        ),
        in_specs=[
            pl.BlockSpec(memory_space=pltpu.SMEM), vm, vm, vm,
            pl.BlockSpec(memory_space=pl.ANY), vm,
        ],
        out_specs=(vm, vm, vm, vm),
        scratch_shapes=[
            V((3, D, 256), BF16),
            V((NP, 16, PC), BF16),
            V((NP, 16, PC), BF16),
            V((NP, 16, PC), BF16),
            V((8, 128), jnp.int32),
            V((NP, 8, 128), jnp.int32),
            V(big, BF16),
            V(big, BF16),
            V((NP, 16, PC), F32),
            V((3, 256, 256), F32),
            V((8, 3, 2, 256, HD), BF16),
            V((8, 2, PC, 256), BF16),
            V(big, BF16),
            V((NP, 8, 16, PC), BF16),
            V((NP, 8, 16, PC), BF16),
            V((NP, 4, 16, PC), BF16),
            V((NP, 4, 16, PC), BF16),
            V((3, NP, 16, PC), BF16),
            V((3, 2, PC, 256), F32),
            V((3, PC, 256), BF16),
            V((3, 2, 192, 256), BF16),
            V((3, PC, 256), BF16),
            V((NP, 8, PC), F32),
            V((NP, 8, PC), F32),
            V((8, PC), F32),
            V((NP, 8, PC), F32),
            V((8, PC), F32),
            V((NP, 8, PC), F32),
            dma((4,)),
            dma((1,)),
            dma((2, 16)),
            dma((2, 16)),
            dma((2, 16)),
            dma((2, 2, 8)),
            dma((2, 4, 8)),
            dma((2, 4, 8)),
            dma((2, 2, 4, 3, 2)),
            dma((2, 4)),
            dma((2, 4)),
            dma((2, 4, 4)),
            dma((2, 3, 4)),
            dma((2, 16)),
            dma((2, 16)),
            dma((2, 16)),
        ],
        compiler_params=pltpu.CompilerParams(
            collective_id=0, has_side_effects=True, vmem_limit_bytes=60 * 1024 * 1024
        ),
    )(
        block_order,
        tokens.reshape(16, D),
        segment_ids,
        layer_norm_gain.reshape(NP, PC),
        jnp.transpose(w_proj, (1, 0, 2)),
        d_attended,
    )
    return att, tbg.reshape(2, 8, D), jnp.transpose(dproj, (1, 0, 2)), gg.reshape(D)


def solution(mesh):
    placed = (P("dp", "mp", None), P("dp", None), P(), P(), P(None, None, "mp"), P("dp", "mp"))
    return jax.shard_map(
        per_device,
        mesh=mesh,
        in_specs=placed,
        out_specs=(P("dp", "mp"), P("dp", "mp", None), P("dp", None, "mp"), P()),
        check_vma=False,
    )
```

time: 579 us -> 118 us (0.20)
  waiting for transfers between devices: 365 us -> 0 us
  blocking collectives: 121 us -> 0 us
  Pallas kernels: 0 us -> 109 us
  matrix products: 37.3 us -> 0 us
  local copies, waits for them, and re-layouts: 25.4 us -> 7.8 us
  between operations: 14.5 us -> 0.64 us
  other arithmetic: 13.5 us -> 0 us
    reduce_scatter x1 -> x0, waiting for transfers between devices: 152 us -> none  [per_device(): lax.psum_scatter(jnp.einsum('btd,btcf->dcf', part, dqkv, preferred_elemen...]
    unnamed x5 -> x0, waiting for transfers between devices: 116 us -> none
    pallas_call x0 -> x1, Pallas kernels: none -> 109 us  [per_device(): pl.pallas_call(kernel, out_shape=(jax.ShapeDtypeStruct((256, 256), BF16),...]
    all_gather x2 -> x0, waiting for transfers between devices: 97.2 us -> none  [the longest x1 97.2 us: per_device(): part_rows = lax.all_gather(tokens, 'dp', axis=0, tiled=True)]
    psum x1 -> x0, blocking collectives: 82.4 us -> none  [per_device(): lax.psum(jnp.sum(normalized_gradient * centered_input_local, axis=(0, 1))...]
    all_gather x1 -> x0, blocking collectives: 38.5 us -> none  [per_device(): part_segs = lax.all_gather(segment_ids, 'dp', axis=0, tiled=True)]
    dot_general x10 -> x0, matrix products: 37.3 us -> none  [the longest x1 8.5 us: per_device(): jnp.einsum('btd,dcf->btcf', normalized_input, w_proj, preferred_element_t...]
    reduce_sum x5 -> x0, other arithmetic: 9.46 us -> none  [the longest x2 4.71 us: layer_statistics(): jnp.mean(center * center, axis=-1, keepdims=True) + 1e-06]
  transfers between devices with their start and end apart: 4 -> 0, of which waited for: 3 -> 0; matrix products, arithmetic and copies ran while one was open for 3% -> 0% of each run, Pallas kernels for 0% -> 0%
where the time goes in v1:
time: 118 us; the launch traced here: 117 us
  Pallas kernels  109 us (92%)
  local copies, waits for them, and re-layouts  7.8 us (7%)
    pallas_call x1, Pallas kernels, per_device(): pl.pallas_call(kernel, out_shape=(jax.ShapeDtypeStruct((256, 256), BF16),...  109 us
    unnamed x3, local copies, waits for them, and re-layouts  5.1 us

profile of v1, /device:TPU:8, one launch (start us, length us, event | category | flops | bytes accessed | tf_op | source)
XLA Modules:
  0.0 117.3 jit_solution(5959842823345903241)
XLA Ops:
  0.6 1.4 %reshape.21.gain = f32[16,384]{1,0:T(8,128)} reshape(f32[6144]{0:T(1024)} %param.9) | data formatting | bytes 49152 | tf_op jit(solution)/shard_map/reshape | solution.py:630
  2.0 108.9 %shard_map.93 = (bf16[256,256]{1,0:T(8,128)(2,1)}, bf16[16,6144]{1,0:T(8,128)(2,1)}, bf16[3,384,256]{2,1,0:T(8,128)(2,1)}, f32[16,384]{1,0:T(8,128)}) custom-call(s32[32]{0:T(128)} %order.1, bf16[16,6144]{1,0:T(8,128)(2,1)} %bitcast.7, s32[2,128]{1,0:T(2,128)} %seg.1, f32[16,384]{1,0:T(8,128)} %reshape.21.gain, bf16[3,6144,256]{2,1,0:T(8,128)(2,1)} %bitcast.4, ...), custom_call_target="tpu_custom_call" | custom-call | tf_op jit(solution)/shard_map/pallas_call | solution.py:564
  110.9 1.3 %reshape.23 = f32[6144]{0:T(1024)} reshape(f32[16,384]{1,0:T(8,128)} %get-tuple-element.11) | data formatting | bytes 49152 | tf_op jit(solution)/shard_map/reshape | solution.py:634
  112.2 1.6 %copy.13 = bf16[256,256]{1,0:T(8,128)(2,1)} copy(bf16[256,256]{1,0:T(8,128)(2,1)} %get-tuple-element.16) | data formatting | bytes 262144
  113.8 1.6 %copy.14 = bf16[2,8,6144]{2,1,0:T(8,128)(2,1)} copy(bf16[2,8,6144]{2,1,0:T(8,128)(2,1)} %bitcast.6) | data formatting | bytes 393216
  115.4 1.9 %copy.15 = bf16[384,3,256]{2,0,1:T(8,128)(2,1)} copy(bf16[384,3,256]{2,0,1:T(8,128)(2,1)} %bitcast.5) | data formatting | bytes 1179648

commit v2 on v0

v2 whole, which is shorter than its diff:
```python
import jax
import jax.numpy as jnp
from jax import lax
from jax.experimental import pallas as pl
from jax.experimental.pallas import tpu as pltpu
from jax.sharding import PartitionSpec as P

D = 6144
HD = 128
PC = 384
NC = 2
NP = 16
F32 = jnp.float32
BF16 = jnp.bfloat16
MESH = pl.DeviceIdType.MESH
CHUNKS = ((0, 2), (0, 0), (0, 1), (1, 2), (1, 0), (1, 1))


def dot(a, b, ca=1, cb=0):
    return lax.dot_general(a, b, (((ca,), (cb,)), ((), ())), preferred_element_type=F32)


def hops_of(way, i):
    return 4 if way == i % 2 else 3


def kernel(
    order, tok, seg, gain_ref, w_hbm, datt,
    att_o, tbg_o, dproj_o, gg_o,
    wv, r1, r2s, r2, segp, sega, gn, nrm, gat, nrow, nsb, xh, proj, zb, nt,
    dnb, rsa, b1, rsb, b2, rsc, rsx, b3, rsy,
    acc, ysnd, fin, gp, gs, ga,
    wsem, lsem, r1sem, r2sem, sgsem, nasem, gasem, nssem, zsem, rasem, rbsem, rcsem, rxsem, rysem, ysem,
    gsem,
):
    dp = lax.axis_index("dp")
    mp = lax.axis_index("mp")
    yh, z = dp // 8, dp % 8
    yl, x, core = mp // 8, (mp // 2) % 4, mp % 2

    def mpid(a, b, c):
        return a * 8 + b * 2 + c

    def mp_of(slot):
        return mpid((slot // 4) % 2, slot % 4, slot // 8)

    sg = core * 8 + yl * 4 + x
    sib = (dp, mpid(yl, x, 1 - core))
    yn = (dp, mpid(1 - yl, x, core))
    xp = (dp, mpid(yl, (x + 1) % 4, core))
    xm = (dp, mpid(yl, (x + 3) % 4, core))
    xo = (dp, mpid(yl, (x + 2) % 4, core))
    zp = (yh * 8 + (z + 1) % 8, mp)
    zm = (yh * 8 + (z + 7) % 8, mp)
    yo = ((1 - yh) * 8 + z, mp)

    def rc(src, dst, sems, dev):
        ss, rs = sems
        return pltpu.make_async_remote_copy(
            src_ref=src, dst_ref=dst, send_sem=ss, recv_sem=rs, device_id=dev, device_id_type=MESH
        )

    def far_first(t):
        half = (t % 8 + 1) // 2
        o = jnp.where(t % 2 == 1, 4 - half, 4 + half) % 8
        return (1 - t // 8) * 8 + o

    def dp_to(i):
        return jnp.where(i >= 8, 1 - yh, yh) * 8 + (z + i) % 8

    def dp_from(i):
        return jnp.where(i >= 8, 1 - yh, yh) * 8 + (z + 16 - i) % 8

    pend = []

    def send(src, dst, sems, dev):
        rc(src, dst, sems, dev).start()
        pend.append((src, dst, sems, dev))

    def got(dst, sems):
        rc(dst, dst, sems, sib).wait_recv()

    wcp = [
        pltpu.make_async_copy(
            w_hbm.at[:, pl.ds(k * 1536, 1536)], wv.at[:, pl.ds(k * 1536, 1536)], wsem.at[k]
        )
        for k in range(4)
    ]
    for cp in wcp:
        cp.start()

    barrier = pltpu.get_barrier_semaphore()

    def greet(t, _):
        pl.semaphore_signal(
            barrier, inc=1, device_id=(dp_to(far_first(t)), mp), device_id_type=MESH
        )
        pl.semaphore_signal(
            barrier, inc=1, device_id=(dp, mp_of((sg + t + 1) % 16)), device_id_type=MESH
        )
        return _

    lax.fori_loop(0, 15, greet, 0)
    segp[...] = jnp.zeros_like(segp)
    segp[0:2, :] = seg[...]
    for j in range(NP):
        gn[j : j + 1, :] = jnp.concatenate(
            [gain_ref[3 * j + n : 3 * j + n + 1, :] for n in range(3)], axis=1
        )
    pl.semaphore_wait(barrier, 30)

    def cols(j):
        return pl.ds(pl.multiple_of(j * PC, 128), PC)

    def r1_copy(i):
        d = dp_to(i)
        return rc(tok.at[:, cols(d)], r1.at[dp], (r1sem.at[0, i], r1sem.at[1, i]), (d, mp))

    def sg_copy(i):
        return rc(segp, sega.at[dp], (sgsem.at[0, i], sgsem.at[1, i]), (dp_to(i), mp))

    def r1_send(t, _):
        r1_copy(far_first(t)).start()
        return _

    lax.fori_loop(0, 15, r1_send, 0)
    own = pltpu.make_async_copy(tok.at[:, cols(dp)], r1.at[dp], lsem.at[0])
    own.start()
    sega[dp] = segp[...]

    def source(i):
        s, r = i >> 3, i & 7
        m = ((s >> 2) & 1) * 8 + (s & 3) * 2 + (s >> 3)
        return m * 8 + r

    ri = lax.broadcasted_iota(jnp.int32, (128, 128), 0)
    ci = lax.broadcasted_iota(jnp.int32, (128, 128), 1)
    perm = jnp.where(source(ri) == ci, 1.0, 0.0).astype(BF16)
    perm_t = jnp.where(source(ci) == ri, 1.0, 0.0).astype(BF16)

    own.wait()

    def r1_wait(i, _):
        got(r1.at[dp_from(i)], (r1sem.at[0, i], r1sem.at[1, i]))
        return _

    lax.fori_loop(1, 16, r1_wait, 0)

    def half_of(p):
        b = order[p]
        t = r1[b >> 1].astype(F32)
        return jnp.where((b & 1) == 1, t[8:16], t[0:8])

    def pick(d):
        return jnp.concatenate([half_of(2 * d), half_of(2 * d + 1)], axis=0).astype(BF16)

    def r2_copy(i):
        d = dp_to(i)
        return rc(r2s.at[d], r2.at[dp], (r2sem.at[0, i], r2sem.at[1, i]), (d, mp))

    def r2_send(t, _):
        i = far_first(t)
        d = dp_to(i)
        r2s[d] = pick(d)
        r2_copy(i).start()
        return _

    lax.fori_loop(0, 15, r2_send, 0)
    r2[dp] = pick(dp)

    def sg_send(i, _):
        sg_copy(i).start()
        return _

    lax.fori_loop(1, 16, sg_send, 0)

    def sg_wait(i, _):
        got(sega.at[dp_from(i)], (sgsem.at[0, i], sgsem.at[1, i]))
        return _

    def ids_of(p):
        b = order[p]
        t = sega[b >> 1].astype(F32)
        return jnp.where((b & 1) == 1, t[1:2], t[0:1])

    def same_image(b):
        ids = jnp.broadcast_to(ids_of(2 * dp + b), (8, 128)).astype(BF16)
        return dot(perm, ids, 1, 1)[:, 0:1] == dot(ids, perm_t)[0:1]

    def r2_wait(i, _):
        got(r2.at[dp_from(i)], (r2sem.at[0, i], r2sem.at[1, i]))
        return _

    lax.fori_loop(1, 16, r2_wait, 0)

    rows = r2[...].astype(F32)
    mean = jnp.sum(jnp.sum(rows, axis=0), axis=-1, keepdims=True) * (1.0 / D)
    cen = rows - mean[None]
    var = jnp.sum(jnp.sum(cen * cen, axis=0), axis=-1, keepdims=True) * (1.0 / D)
    rstd = lax.rsqrt(var + 1e-06)
    xhat = cen * rstd[None]
    normed = [xhat[j] * gn[j : j + 1, :] for j in range(NP)]
    for b in range(2):
        half = slice(8 * b, 8 * b + 8)
        for j in range(8):
            both = jnp.concatenate([normed[j][half], normed[j + 8][half]], axis=0)
            gat[8 * b + j, sg] = both.astype(BF16)

    def gather(buf, sems, chunks):
        n = NP // chunks

        def at(k, slot):
            return buf.at[pl.ds(n * k, n), slot]

        def slot(a, b):
            return core * 8 + a * 4 + b

        def sm(k, m):
            return (sems.at[0, k, m], sems.at[1, k, m])

        def go(k, a, b, m, dev):
            ref = at(k, slot(a, b))
            send(ref, ref, sm(k, m), dev)

        def have(k, a, b, m):
            got(at(k, slot(a, b)), sm(k, m))

        x1, x2, x3 = (x + 1) % 4, (x + 2) % 4, (x + 3) % 4

        def stage0(k):
            go(k, yl, x, 0, yn)

        def stage1(k):
            for m, dev in ((1, xp), (2, xm), (3, xo)):
                go(k, yl, x, m, dev)

        def stage2(k):
            have(k, 1 - yl, x, 0)
            for m, dev in ((4, xp), (5, xm), (6, xo)):
                go(k, 1 - yl, x, m, dev)

        def stage4(k):
            for m, a, b in ((1, yl, x3), (2, yl, x1), (3, yl, x2)):
                have(k, a, b, m)
                have(k, 1 - a, b, m + 3)
            ref = buf.at[pl.ds(n * k, n), pl.ds(core * 8, 8)]
            send(ref, ref, sm(k, 7), sib)

        def stage5(k):
            got(buf.at[pl.ds(n * k, n), pl.ds((1 - core) * 8, 8)], sm(k, 7))

        return stage0, stage1, stage2, stage4, stage5

    G0, G1, G2, G4, G5 = gather(gat, gasem, 4)
    N0, N1, N2, N4, N5 = gather(nsb, nssem, NC)
    for k in range(4):
        G0(k)
    G1(0)
    G1(1)
    xh[...] = xhat
    for j in range(NP):
        nrm[j % 8, j // 8] = normed[j].astype(BF16)

    def na_copy(o):
        t = (z + o) % 8
        return rc(
            nrm.at[t], nsb.at[pl.ds(2 * z, 2), sg], (nasem.at[0, o], nasem.at[1, o]),
            (yh * 8 + t, mp),
        )

    def na_send(o, _):
        na_copy(o).start()
        return _

    G2(0)
    G2(1)
    G1(2)
    G2(2)
    lax.fori_loop(1, 8, na_send, 0)
    for i in range(2):
        nsb[2 * z + i, sg] = nrm[z, i]

    def na_wait(o, _):
        s = (z + 8 - o) % 8
        got(nsb.at[pl.ds(2 * s, 2), sg], (nasem.at[0, o], nasem.at[1, o]))
        return _

    lax.fori_loop(1, 16, sg_wait, 0)
    same = [same_image(b) for b in range(2)]
    g = [dot(perm, datt[128 * b : 128 * b + 128, :]).astype(BF16) for b in range(2)]
    G4(0)
    G1(3)
    G2(3)
    G4(1)
    for cp in wcp:
        cp.wait()

    def project(b, n):
        G5(2 * b + n)
        for q in range(2):
            j = 4 * n + 2 * q
            u = [gat[8 * b + j + i].astype(F32) for i in range(2)]
            for m in range(2):
                e = [t[:, 8 * m : 8 * m + 8].reshape(128, PC).astype(BF16) for t in u]
                p = j + 8 * m
                nrow[p, 128 * b : 128 * b + 128] = e[0]
                nrow[p + 1, 128 * b : 128 * b + 128] = e[1]
                lhs = jnp.concatenate(e, axis=1)
                for c in range(3):
                    t = dot(lhs, wv[c, p * PC : (p + 2) * PC, :])
                    proj[c] = t if p == 0 else proj[c] + t

    scale = HD ** (-0.5)

    def z_refs(way, hop, i):
        b, c = CHUNKS[i]
        return zb.at[(z + (8 - hop if way == 0 else hop)) % 8, b, c]

    def z_send(way, hop, i):
        ref = z_refs(way, hop, i)
        send(
            ref, ref, (zsem.at[0, way, hop, i], zsem.at[1, way, hop, i]), zp if way == 0 else zm
        )

    def z_have(way, hop, i):
        got(z_refs(way, hop, i), (zsem.at[0, way, hop - 1, i], zsem.at[1, way, hop - 1, i]))

    def w(hop, i):
        for way in range(2):
            n = hops_of(way, i)
            if hop <= n:
                z_have(way, hop, i)
            if hop < n:
                z_send(way, hop, i)

    def first(i):
        z_send(0, 0, i)
        z_send(1, 0, i)

    def attend(b):
        lanes = [slice(h * HD, (h + 1) * HD) for h in range(2)]
        qkv = [[proj[c, :, lanes[h]].astype(BF16) for c in range(3)] for h in range(2)]
        gh = [g[b][:, lanes[h]] for h in range(2)]
        probs, pb = [], []
        for h in range(2):
            q, k, v = qkv[h]
            s = jnp.where(same[b], dot(q, k, 1, 1) * scale, -1e30)
            e = jnp.exp(s - jnp.max(s, axis=-1, keepdims=True))
            probs.append(e / jnp.sum(e, axis=-1, keepdims=True))
            pb.append(probs[h].astype(BF16))

        def put(i, vals):
            for h in range(2):
                zb[z, b, CHUNKS[i][1], h] = vals[h].astype(BF16)
            if i <= 3:
                first(i)

        put(3 * b, [dot(pb[h], gh[h], 0, 0) for h in range(2)])
        ds = []
        for h in range(2):
            dprob = dot(gh[h], qkv[h][2], 1, 1)
            delta = jnp.sum(probs[h] * dprob, axis=-1, keepdims=True)
            ds.append((probs[h] * (dprob - delta)).astype(BF16))
        put(3 * b + 1, [dot(ds[h], qkv[h][1]) * scale for h in range(2)])
        put(3 * b + 2, [dot(ds[h], qkv[h][0], 0, 0) * scale for h in range(2)])
        outs = [dot(pb[h], qkv[h][2]).astype(BF16) for h in range(2)]
        out = dot(perm_t, jnp.concatenate(outs, axis=1))
        att_o[128 * b : 128 * b + 128, :] = out.astype(BF16)

    project(0, 0)
    project(0, 1)
    attend(0)
    G4(2)
    lax.fori_loop(1, 8, na_wait, 0)
    for k in range(NC):
        N0(k)
    N1(0)
    w(1, 0)
    G4(3)
    N1(1)
    N2(0)
    w(1, 1)
    project(1, 0)
    N2(1)
    w(1, 2)
    project(1, 1)
    w(2, 0)
    w(2, 1)
    attend(1)

    def part(c):
        return jnp.concatenate(
            [jnp.concatenate([zb[z, b, c, 0], zb[z, b, c, 1]], axis=1) for b in range(2)], axis=0
        )

    dq = [part(c) for c in range(3)]

    def dn_step(k):
        def body(j, _):
            at = pl.ds(pl.multiple_of(j * PC, 128), PC)
            t = dot(dq[0], wv[0, at, :], 1, 1)
            t = t + dot(dq[1], wv[1, at, :], 1, 1)
            t = t + dot(dq[2], wv[2, at, :], 1, 1)
            t = t.astype(BF16).astype(F32)
            gp[j] = jnp.sum((t * nrow[j].astype(F32)).reshape(32, 8, PC), axis=0)
            t = t.reshape(2, 16, 8, PC)
            dnb[j] = jnp.concatenate([t[0], t[1]], axis=1).astype(BF16)
            return _

        lax.fori_loop(4 * k, 4 * k + 4, body, 0)
        send(
            dnb.at[pl.ds(4 * k, 4), pl.ds((1 - core) * 8, 8)], rsa.at[pl.ds(4 * k, 4)],
            (rasem.at[0, k], rasem.at[1, k]), sib,
        )

    def s2(k):
        got(rsa.at[pl.ds(4 * k, 4)], (rasem.at[0, k], rasem.at[1, k]))
        for j in range(4 * k, 4 * k + 4):
            mine = dnb[j, pl.ds(core * 8, 8)].astype(F32)
            b1[j] = (mine + rsa[j].astype(F32)).astype(BF16).reshape(2, 4, 16, PC)
        if k < 2:
            send(
                b1.at[pl.ds(4 * k, 4), 1 - yl], rsb.at[pl.ds(4 * k, 4)],
                (rbsem.at[0, k], rbsem.at[1, k]), yn,
            )
        else:
            for o, dev in ((1, xp), (2, xo), (3, xm)):
                send(
                    b1.at[pl.ds(4 * k, 4), :, (x + o) % 4], rsx.at[o - 1, k - 2],
                    (rxsem.at[0, o, k - 2], rxsem.at[1, o, k - 2]), dev,
                )

    def s3(k):
        if k < 2:
            got(rsb.at[pl.ds(4 * k, 4)], (rbsem.at[0, k], rbsem.at[1, k]))
            for j in range(4 * k, 4 * k + 4):
                b2[j] = (b1[j, yl].astype(F32) + rsb[j].astype(F32)).astype(BF16)
            for o, dev in ((1, xp), (2, xo), (3, xm)):
                send(
                    b2.at[pl.ds(4 * k, 4), (x + o) % 4], rsc.at[o - 1, pl.ds(4 * k, 4)],
                    (rcsem.at[0, o, k], rcsem.at[1, o, k]), dev,
                )
        else:
            at = pl.ds(4 * (k - 2), 4)
            for o in range(1, 4):
                got(rsx.at[o - 1, k - 2], (rxsem.at[0, o, k - 2], rxsem.at[1, o, k - 2]))
            for j in range(4):
                t = b1[4 * k + j, :, x].astype(F32)
                for o in range(3):
                    t = t + rsx[o, k - 2, j].astype(F32)
                b3[4 * (k - 2) + j] = t.astype(BF16)
            send(
                b3.at[at, 1 - yl], rsy.at[at], (rysem.at[0, k - 2], rysem.at[1, k - 2]), yn
            )

    def rows_out():
        for k in range(2):
            for o in range(1, 4):
                got(rsc.at[o - 1, pl.ds(4 * k, 4)], (rcsem.at[0, o, k], rcsem.at[1, o, k]))
            got(rsy.at[pl.ds(4 * k, 4)], (rysem.at[0, k], rysem.at[1, k]))
        parts = []
        for j in range(NP):
            if j < 8:
                t = b2[j, x].astype(F32)
                for o in range(3):
                    t = t + rsc[o, j].astype(F32)
            else:
                t = b3[j - 8, yl].astype(F32) + rsy[j - 8].astype(F32)
            parts.append(t * gn[j : j + 1, :])
        m1 = sum(jnp.sum(parts[j], axis=-1, keepdims=True) for j in range(NP)) * (1.0 / D)
        m2 = sum(jnp.sum(parts[j] * xh[j], axis=-1, keepdims=True) for j in range(NP)) * (1.0 / D)
        for j in range(NP):
            t = rstd * (parts[j] - m1 - xh[j] * m2)
            tbg_o[:, j * PC : (j + 1) * PC] = t.astype(BF16)

    kinds = (
        sib, yn, (dp, mpid(yl, x + 1 - 2 * (x % 2), core)), xo,
        (yh * 8 + z + 1 - 2 * (z % 2), mp), (yh * 8 + z + 2 - 4 * ((z // 2) % 2), mp),
        (yh * 8 + (z + 4) % 8, mp), ((1 - yh) * 8 + z, mp),
    )

    def gain(n):
        if n == 0:
            for j in range(NP):
                t = jnp.sum(gp[j], axis=0, keepdims=True)
                for m in range(3):
                    gs[0, 3 * j + m : 3 * j + m + 1, :] = t[:, m * 128 : m * 128 + 128]
        else:
            got(ga.at[n - 1], (gsem.at[0, n - 1], gsem.at[1, n - 1]))
            gs[n] = gs[n - 1] + ga[n - 1]
        if n < 8:
            send(gs.at[n], ga.at[n], (gsem.at[0, n], gsem.at[1, n]), kinds[n])
        else:
            gg_o[...] = gs[n] / gain_ref[...]

    def turn(s, _):
        for i in range(2):
            u = nsb[2 * s + i].astype(F32)
            for b in range(2):
                e = u[:, 8 * b : 8 * b + 8].reshape(128, PC).astype(BF16)
                nt[b, i, :, pl.ds(pl.multiple_of(s * 128, 128), 128)] = e.T
        return _

    def dproj(b, c):
        rhs = jnp.concatenate(
            [jnp.concatenate([zb[s, b, c, 0], zb[s, b, c, 1]], axis=1) for s in range(8)], axis=0
        )
        for i in range(2):
            t = dot(nt[b, i], rhs)
            acc[c, i] = t if b == 0 else acc[c, i] + t

    def swap(c):
        ysnd[c] = acc[c, 1 - yh].astype(BF16)
        send(ysnd.at[c], fin.at[c], (ysem.at[0, c], ysem.at[1, c]), yo)

    def finish(c):
        got(fin.at[c], (ysem.at[0, c], ysem.at[1, c]))
        dproj_o[c] = (acc[c, yh] + fin[c].astype(F32)).astype(BF16)

    w(2, 2)
    dn_step(0)
    w(3, 0)
    dn_step(1)
    s2(0)
    w(3, 1)
    w(1, 3)
    first(4)
    dn_step(2)
    s2(1)
    w(3, 2)
    dn_step(3)
    s2(2)
    w(2, 3)
    w(1, 4)
    first(5)
    gain(0)
    s2(3)
    w(4, 0)
    w(4, 1)
    gain(1)
    w(3, 3)
    w(2, 4)
    w(1, 5)
    for k in range(NC):
        N4(k)
    s3(0)
    gain(2)
    w(4, 2)
    s3(1)
    for k in range(NC):
        N5(k)
    lax.fori_loop(0, 8, turn, 0)
    gain(3)
    dproj(0, 2)
    w(4, 3)
    dproj(1, 2)
    swap(2)
    w(3, 4)
    w(2, 5)
    gain(4)
    s3(2)
    dproj(0, 0)
    w(4, 4)
    dproj(1, 0)
    swap(0)
    w(3, 5)
    gain(5)
    s3(3)
    dproj(0, 1)
    gain(6)
    w(4, 5)
    dproj(1, 1)
    swap(1)
    gain(7)
    finish(2)
    rows_out()
    finish(0)
    gain(8)
    finish(1)

    def drain(i, _):
        r1_copy(i).wait_send()
        sg_copy(i).wait_send()
        r2_copy(i).wait_send()
        return _

    lax.fori_loop(1, 16, drain, 0)

    def drain_na(o, _):
        na_copy(o).wait_send()
        return _

    lax.fori_loop(1, 8, drain_na, 0)
    for item in pend:
        rc(*item).wait_send()


def hand_over(*refs):
    for a, b in zip(refs[:4], refs[4:]):
        b[...] = a[...]


def per_device(tokens, segment_ids, block_order, layer_norm_gain, w_proj, d_attended):
    vm = pl.BlockSpec(memory_space=pltpu.VMEM)
    dma = pltpu.SemaphoreType.DMA
    V = pltpu.VMEM
    big = (NP, 16, 16, PC)
    shapes = (
        jax.ShapeDtypeStruct((256, 256), BF16),
        jax.ShapeDtypeStruct((16, D), BF16),
        jax.ShapeDtypeStruct((3, PC, 256), BF16),
        jax.ShapeDtypeStruct((48, 128), F32),
    )
    made = pl.pallas_call(
        kernel,
        out_shape=shapes,
        in_specs=[
            pl.BlockSpec(memory_space=pltpu.SMEM), vm, vm, vm,
            pl.BlockSpec(memory_space=pl.ANY), vm,
        ],
        out_specs=(vm, vm, vm, vm),
        scratch_shapes=[
            V((3, D, 256), BF16),
            V((NP, 16, PC), BF16),
            V((NP, 16, PC), BF16),
            V((NP, 16, PC), BF16),
            V((8, 128), jnp.int32),
            V((NP, 8, 128), jnp.int32),
            V((NP, PC), F32),
            V((8, 2, 16, PC), BF16),
            V(big, BF16),
            V((NP, 256, PC), BF16),
            V(big, BF16),
            V((NP, 16, PC), F32),
            V((3, 128, 256), F32),
            V((8, 2, 3, 2, 128, HD), BF16),
            V((2, 2, PC, 1024), BF16),
            V(big, BF16),
            V((NP, 8, 16, PC), BF16),
            V((NP, 2, 4, 16, PC), BF16),
            V((8, 4, 16, PC), BF16),
            V((8, 4, 16, PC), BF16),
            V((3, 8, 16, PC), BF16),
            V((3, 2, 4, 2, 16, PC), BF16),
            V((8, 2, 16, PC), BF16),
            V((8, 16, PC), BF16),
            V((3, 2, PC, 256), F32),
            V((3, PC, 256), BF16),
            V((3, PC, 256), BF16),
            V((NP, 8, PC), F32),
            V((9, 48, 128), F32),
            V((8, 48, 128), F32),
            dma((4,)),
            dma((1,)),
            dma((2, 16)),
            dma((2, 16)),
            dma((2, 16)),
            dma((2, 8)),
            dma((2, 4, 8)),
            dma((2, NC, 8)),
            dma((2, 2, 4, 6)),
            dma((2, 4)),
            dma((2, 2)),
            dma((2, 4, 2)),
            dma((2, 4, 2)),
            dma((2, 2)),
            dma((2, 3)),
            dma((2, 8)),
        ],
        compiler_params=pltpu.CompilerParams(
            collective_id=0, has_side_effects=True, vmem_limit_bytes=60 * 1024 * 1024
        ),
    )(
        block_order,
        tokens.reshape(16, D),
        segment_ids,
        layer_norm_gain.reshape(48, 128),
        jnp.transpose(w_proj, (1, 0, 2)),
        d_attended,
    )
    att, tbg, dproj, gg = pl.pallas_call(
        hand_over,
        out_shape=shapes,
        in_specs=[vm] * 4,
        out_specs=(vm,) * 4,
    )(*made)
    return att, tbg.reshape(2, 8, D), jnp.transpose(dproj, (1, 0, 2)), gg.reshape(D)


def solution(mesh):
    placed = (P("dp", "mp", None), P("dp", None), P(), P(), P(None, None, "mp"), P("dp", "mp"))
    return jax.shard_map(
        per_device,
        mesh=mesh,
        in_specs=placed,
        out_specs=(P("dp", "mp"), P("dp", "mp", None), P("dp", None, "mp"), P()),
        check_vma=False,
    )
```

time: 579 us -> 99 us (0.17)
  waiting for transfers between devices: 365 us -> 0 us
  blocking collectives: 121 us -> 0 us
  Pallas kernels: 0 us -> 98.2 us
  matrix products: 37.3 us -> 0 us
  local copies, waits for them, and re-layouts: 25.4 us -> 0 us
  between operations: 14.5 us -> 0.64 us
  other arithmetic: 13.5 us -> 0 us
    reduce_scatter x1 -> x0, waiting for transfers between devices: 152 us -> none  [per_device(): lax.psum_scatter(jnp.einsum('btd,btcf->dcf', part, dqkv, preferred_elemen...]
    unnamed x5 -> x0, waiting for transfers between devices: 116 us -> none
    pallas_call x0 -> x2, Pallas kernels: none -> 98.2 us  [the longest x1 96 us: per_device(): pl.pallas_call(kernel, out_shape=shapes, in_specs=[pl.BlockSpec(memory_sp...]
    all_gather x2 -> x0, waiting for transfers between devices: 97.2 us -> none  [the longest x1 97.2 us: per_device(): part_rows = lax.all_gather(tokens, 'dp', axis=0, tiled=True)]
    psum x1 -> x0, blocking collectives: 82.4 us -> none  [per_device(): lax.psum(jnp.sum(normalized_gradient * centered_input_local, axis=(0, 1))...]
    all_gather x1 -> x0, blocking collectives: 38.5 us -> none  [per_device(): part_segs = lax.all_gather(segment_ids, 'dp', axis=0, tiled=True)]
    dot_general x10 -> x0, matrix products: 37.3 us -> none  [the longest x1 8.5 us: per_device(): jnp.einsum('btd,dcf->btcf', normalized_input, w_proj, preferred_element_t...]
    reduce_sum x5 -> x0, other arithmetic: 9.46 us -> none  [the longest x2 4.71 us: layer_statistics(): jnp.mean(center * center, axis=-1, keepdims=True) + 1e-06]
  transfers between devices with their start and end apart: 4 -> 0, of which waited for: 3 -> 0; matrix products, arithmetic and copies ran while one was open for 3% -> 0% of each run, Pallas kernels for 0% -> 0%
where the time goes in v2:
time: 99 us; the launch traced here: 98.9 us
  Pallas kernels  98.2 us (99%)
    pallas_call x1, Pallas kernels, per_device(): pl.pallas_call(kernel, out_shape=shapes, in_specs=[pl.BlockSpec(memory_sp...  96 us
    pallas_call x1, Pallas kernels, per_device(): pl.pallas_call(hand_over, out_shape=shapes, in_specs=[vm] * 4, out_specs=...  2.18 us

profile of v2, /device:TPU:8, one launch (start us, length us, event | category | flops | bytes accessed | tf_op | source)
XLA Modules:
  0.0 98.9 jit_solution(18263862439178671527)
XLA Ops:
  0.6 96.0 %shard_map.93 = (bf16[256,256]{1,0:T(8,128)(2,1)}, bf16[16,6144]{1,0:T(8,128)(2,1)}, bf16[3,384,256]{2,1,0:T(8,128)(2,1)}, f32[48,128]{1,0:T(8,128)}) custom-call(s32[32]{0:T(128)} %order.1, bf16[16,6144]{1,0:T(8,128)(2,1)} %bitcast.7, s32[2,128]{1,0:T(2,128)} %seg.1, f32[48,128]{1,0:T(8,128)} %bitcast.8, bf16[3,6144,256]{2,1,0:T(8,128)(2,1)} %bitcast.6, ...), custom_call_target="tpu_custom_call" | custom-call | tf_op jit(solution)/shard_map/pallas_call | solution.py:614
  96.7 2.2 %shard_map.94 = (bf16[256,256]{1,0:T(8,128)(2,1)}, bf16[16,6144]{1,0:T(8,128)(2,1)}, bf16[3,384,256]{2,1,0:T(8,128)(2,1)}, f32[48,128]{1,0:T(8,128)}) custom-call(bf16[256,256]{1,0:T(8,128)(2,1)} %get-tuple-element.12.refs_0_, bf16[16,6144]{1,0:T(8,128)(2,1)} %get-tuple-element.13.refs_1_, bf16[3,384,256]{2,1,0:T(8,128)(2,1)} %get-tuple-element.14.refs_2_, ...), custom_call_target="tpu_custom_call" | custom-call | tf_op jit(solution)/shard_map/pallas_call | solution.py:681

commit v3 on v2

--- a/solution.py
+++ b/solution.py
@@ -352,7 +352,7 @@
         def put(i, vals):
             for h in range(2):
                 zb[z, b, CHUNKS[i][1], h] = vals[h].astype(BF16)
-            if i <= 3:
+            if i <= 4:
                 first(i)
 
         put(3 * b, [dot(pb[h], gh[h], 0, 0) for h in range(2)])
@@ -375,12 +375,12 @@
     for k in range(NC):
         N0(k)
     N1(0)
+    project(1, 0)
     w(1, 0)
     G4(3)
     N1(1)
     N2(0)
     w(1, 1)
-    project(1, 0)
     N2(1)
     w(1, 2)
     project(1, 1)
@@ -473,10 +473,17 @@
             t = rstd * (parts[j] - m1 - xh[j] * m2)
             tbg_o[:, j * PC : (j + 1) * PC] = t.astype(BF16)
 
+    zl, hi = z % 4, yh * 2 + z // 4
+
+    def hi_dev(n):
+        return ((n // 2) * 8 + (n % 2) * 4 + zl, mp)
+
     kinds = (
-        sib, yn, (dp, mpid(yl, x + 1 - 2 * (x % 2), core)), xo,
-        (yh * 8 + z + 1 - 2 * (z % 2), mp), (yh * 8 + z + 2 - 4 * ((z // 2) % 2), mp),
-        (yh * 8 + (z + 4) % 8, mp), ((1 - yh) * 8 + z, mp),
+        (2, core, lambda n: (dp, mpid(yl, x, n))),
+        (4, zl, lambda n: (yh * 8 + z - zl + n, mp)),
+        (4, hi, hi_dev),
+        (4, x, lambda n: (dp, mpid(yl, n, core))),
+        (2, yl, lambda n: (dp, mpid(n, x, core))),
     )
 
     def gain(n):
@@ -486,10 +493,21 @@
                 for m in range(3):
                     gs[0, 3 * j + m : 3 * j + m + 1, :] = t[:, m * 128 : m * 128 + 128]
         else:
-            got(ga.at[n - 1], (gsem.at[0, n - 1], gsem.at[1, n - 1]))
-            gs[n] = gs[n - 1] + ga[n - 1]
-        if n < 8:
-            send(gs.at[n], ga.at[n], (gsem.at[0, n], gsem.at[1, n]), kinds[n])
+            size, rank, _ = kinds[n - 1]
+            ga[n - 1, rank] = gs[n - 1]
+            for o in range(1, size):
+                got(ga.at[n - 1, (rank + size - o) % size], (gsem.at[0, n - 1, o], gsem.at[1, n - 1, o]))
+            t = ga[n - 1, 0] + ga[n - 1, 1]
+            if size == 4:
+                t = t + ga[n - 1, 2] + ga[n - 1, 3]
+            gs[n] = t
+        if n < 5:
+            size, rank, dev = kinds[n]
+            for o in range(1, size):
+                send(
+                    gs.at[n], ga.at[n, rank], (gsem.at[0, n, o], gsem.at[1, n, o]),
+                    dev((rank + o) % size),
+                )
         else:
             gg_o[...] = gs[n] / gain_ref[...]
 
@@ -524,59 +542,52 @@
     s2(0)
     w(3, 1)
     w(1, 3)
-    first(4)
+    first(5)
     dn_step(2)
     s2(1)
     w(3, 2)
+    w(1, 4)
     dn_step(3)
+    gain(0)
     s2(2)
     w(2, 3)
-    w(1, 4)
-    first(5)
-    gain(0)
+    gain(1)
     s2(3)
     w(4, 0)
     w(4, 1)
-    gain(1)
-    w(3, 3)
-    w(2, 4)
-    w(1, 5)
     for k in range(NC):
         N4(k)
+    w(1, 5)
     s3(0)
-    gain(2)
-    w(4, 2)
-    s3(1)
+    w(2, 4)
     for k in range(NC):
         N5(k)
-    lax.fori_loop(0, 8, turn, 0)
-    gain(3)
+    lax.fori_loop(0, 4, turn, 0)
+    w(3, 3)
+    gain(2)
+    s3(1)
+    lax.fori_loop(4, 8, turn, 0)
+    w(2, 5)
     dproj(0, 2)
+    w(4, 2)
+    w(3, 4)
     w(4, 3)
     dproj(1, 2)
     swap(2)
-    w(3, 4)
-    w(2, 5)
-    gain(4)
     s3(2)
+    gain(3)
+    w(3, 5)
     dproj(0, 0)
     w(4, 4)
     dproj(1, 0)
     swap(0)
-    w(3, 5)
-    gain(5)
     s3(3)
     dproj(0, 1)
-    gain(6)
+    gain(4)
     w(4, 5)
     dproj(1, 1)
     swap(1)
-    gain(7)
-    finish(2)
     rows_out()
-    finish(0)
-    gain(8)
-    finish(1)
 
     def drain(i, _):
         r1_copy(i).wait_send()
@@ -591,7 +602,13 @@
         return _
 
     lax.fori_loop(1, 8, drain_na, 0)
-    for item in pend:
+    for item in pend[:-3]:
+        rc(*item).wait_send()
+    finish(2)
+    finish(0)
+    gain(5)
+    finish(1)
+    for item in pend[-3:]:
         rc(*item).wait_send()
 
 
@@ -648,8 +665,8 @@
             V((3, PC, 256), BF16),
             V((3, PC, 256), BF16),
             V((NP, 8, PC), F32),
-            V((9, 48, 128), F32),
-            V((8, 48, 128), F32),
+            V((6, 48, 128), F32),
+            V((5, 4, 48, 128), F32),
             dma((4,)),
             dma((1,)),
             dma((2, 16)),
@@ -665,7 +682,7 @@
             dma((2, 4, 2)),
             dma((2, 2)),
             dma((2, 3)),
-            dma((2, 8)),
+            dma((2, 5, 4)),
         ],
         compiler_params=pltpu.CompilerParams(
             collective_id=0, has_side_effects=True, vmem_limit_bytes=60 * 1024 * 1024

time: 99 us -> 97.6 us (0.986); the launches traced: 98.9 us -> 96.3 us
  Pallas kernels: 98.2 us -> 95.7 us
    pallas_call x1, Pallas kernels: 96 us -> 93.5 us  [per_device(): pl.pallas_call(kernel, out_shape=shapes, in_specs=[pl.BlockSpec(memory_sp...]
where the time goes in v3:
time: 97.6 us; the launch traced here: 96.3 us
  Pallas kernels  95.7 us (98%)
    pallas_call x1, Pallas kernels, per_device(): pl.pallas_call(kernel, out_shape=shapes, in_specs=[pl.BlockSpec(memory_sp...  93.5 us
    pallas_call x1, Pallas kernels, per_device(): pl.pallas_call(hand_over, out_shape=shapes, in_specs=[vm] * 4, out_specs=...  2.18 us

profile of v3, /device:TPU:8, one launch (start us, length us, event | category | flops | bytes accessed | tf_op | source)
XLA Modules:
  0.0 96.3 jit_solution(899059298163588742)
XLA Ops:
  0.6 93.5 %shard_map.93 = (bf16[256,256]{1,0:T(8,128)(2,1)}, bf16[16,6144]{1,0:T(8,128)(2,1)}, bf16[3,384,256]{2,1,0:T(8,128)(2,1)}, f32[48,128]{1,0:T(8,128)}) custom-call(s32[32]{0:T(128)} %order.1, bf16[16,6144]{1,0:T(8,128)(2,1)} %bitcast.7, s32[2,128]{1,0:T(2,128)} %seg.1, f32[48,128]{1,0:T(8,128)} %bitcast.8, bf16[3,6144,256]{2,1,0:T(8,128)(2,1)} %bitcast.6, ...), custom_call_target="tpu_custom_call" | custom-call | tf_op jit(solution)/shard_map/pallas_call | solution.py:631
  94.1 2.2 %shard_map.94 = (bf16[256,256]{1,0:T(8,128)(2,1)}, bf16[16,6144]{1,0:T(8,128)(2,1)}, bf16[3,384,256]{2,1,0:T(8,128)(2,1)}, f32[48,128]{1,0:T(8,128)}) custom-call(bf16[256,256]{1,0:T(8,128)(2,1)} %get-tuple-element.12.refs_0_, bf16[16,6144]{1,0:T(8,128)(2,1)} %get-tuple-element.13.refs_1_, bf16[3,384,256]{2,1,0:T(8,128)(2,1)} %get-tuple-element.14.refs_2_, ...), custom_call_target="tpu_custom_call" | custom-call | tf_op jit(solution)/shard_map/pallas_call | solution.py:698
